TPU v7x, 256 devices: a whole 4x4x8 slice. The times are simulated.
256 devices in a mesh: gy: 32 (over x, y, core), gz: 8 (over z).
Axes of the slice: x: 4, y: 4, z: 8, core: 2. Of those that a mesh axis runs over, the one named last changes fastest.
Arguments:
- spectrum: bfloat16 [2, 8, 8192, 1536], P(None, 'gz', 'gy'), may hold values from -2000 to 2000
- layer_index: int32 [1536], replicated, may hold values from 0 to 7, as said below
- y_bounds: int32 [33], replicated, may hold values from 0 to 8192, as said below
- z_bounds: int32 [9], replicated, may hold values from 0 to 1536, as said below
- vp: bfloat16 [10240, 15360], P('gy', 'gz'), may hold values from 3 to 6
- vs: bfloat16 [10240, 15360], P('gy', 'gz'), may hold values from 1.5 to 3.5
- rho: bfloat16 [10240, 15360], P('gy', 'gz'), may hold values from 2 to 2.796875
Outputs:
- new_vp: float32 [10240, 15360], P('gy', 'gz')
- new_vs: float32 [10240, 15360], P('gy', 'gz')
- new_rho: float32 [10240, 15360], P('gy', 'gz')
Inputs may be any that keep to these rules, and one draw needn't show every extreme that they name: `layer_index`: never falls with depth; the first cell is in layer 0 and the last in layer 7. `y_bounds`: starts at 0 and ends at 8192; each brick row spans from 192 to 320 cells, and in every draw some row spans exactly 320 and some exactly 192. `z_bounds`: starts at 0 and ends at 1536; each brick column spans from 3 * 1536 // (4 * 8) to 240 cells, and in every draw some column spans exactly 240 and some exactly the least.
All inputs are finite; a program needn't handle non-finite values.
Results may differ from a plain program's by a relative error of at most 0.0013.
Values may be sent and summed in bfloat16 or wider, within the bound.
No kernel may reach another device: no remote copies, remote signals or barrier semaphores. Data moves between devices by JAX's collectives and lax.ppermute only.
A program may use at most 128 MiB of HBM per device.

v0:
```python
import functools
import math

import jax
import jax.numpy as jnp
import numpy as np
from jax import lax
from jax.experimental import pallas as pl
from jax.experimental.pallas import tpu as pltpu
from jax.sharding import PartitionSpec as P

LAYERS = 8
CORRELATION = 8.0
HURST_EXPONENT = 0.1
SPREAD_SIGMA = 0.1
DENSITY_GAIN = 0.8
EPSILON = 1e-06

NY, NZ, X = 8192, 1536, 8
GY, GZ = 32, 8
ROWS = NY // GY
CHUNK = 64
BAND = NZ // GY
YCAP, ZCAP = 320, 240
INNER = 128
OUTER = NZ // INNER
RADIX = 16
LONG = NY // RADIX
STEP = YCAP // RADIX + 1
PER = 6
WIDE = 384
MANY = 8
TILES = WIDE // 128
DEEP = 8
PERIOD = GY * DEEP
f32, bf16 = jnp.float32, jnp.bfloat16
MIB = 1024 * 1024


def inner_table():
    angle = 2.0 * np.pi * (np.outer(np.arange(INNER), np.arange(INNER)) % INNER) / INNER
    c, s = np.cos(angle), np.sin(angle)
    return np.block([[c, -s], [s, c]]).astype(bf16)


def depth_twist():
    angle = 2.0 * np.pi * np.outer(np.arange(OUTER), np.arange(INNER)) / NZ
    return np.stack([np.cos(angle), np.sin(angle)], axis=1).reshape(2 * OUTER, INNER).astype(np.float32)


def y_table():
    angle = 2.0 * np.pi * (np.outer(np.arange(LONG), np.arange(LONG)) % LONG) / LONG
    full = np.concatenate([np.cos(angle), -np.sin(angle)], axis=0).astype(bf16)
    return np.ascontiguousarray(full.reshape(2 * LONG, LONG // 256, 256).transpose(1, 0, 2))


def y_twist():
    y1 = np.arange(RADIX)
    angle = 2.0 * np.pi * np.outer(y1 - RADIX * STEP * (y1 % PER), np.arange(LONG)) / NY
    both = np.stack([np.cos(angle), np.sin(angle)], axis=1).astype(np.float32)
    split = both.reshape(2 * RADIX, LONG // ROWS, ROWS).transpose(1, 0, 2)
    return np.ascontiguousarray(split)


def four(a):
    (r0, i0), (r1, i1), (r2, i2), (r3, i3) = a
    sr, si, dr, di = r0 + r2, i0 + i2, r0 - r2, i0 - i2
    tr, ti, er, ei = r1 + r3, i1 + i3, r1 - r3, i1 - i3
    return [(sr + tr, si + ti), (dr - ei, di + er), (sr - tr, si - ti), (dr + ei, di - er)]


def three(a):
    (r0, i0), (r1, i1), (r2, i2) = a
    tr, ti = r1 + r2, i1 + i2
    half = math.sqrt(3.0) / 2.0
    er, ei = (r1 - r2) * half, (i1 - i2) * half
    mr, mi = r0 - 0.5 * tr, i0 - 0.5 * ti
    return [(r0 + tr, i0 + ti), (mr - ei, mi + er), (mr + ei, mi - er)]


def twelve(a):
    quarter = [four([a[(4 * i + 3 * j) % 12] for j in range(4)]) for i in range(3)]
    out = [None] * 12
    for v in range(4):
        for u, value in enumerate(three([quarter[i][v] for i in range(3)])):
            out[next(q for q in range(12) if q % 3 == u and q % 4 == v)] = value
    return out


def sixteen(a):
    first = []
    for b in range(4):
        column = four(a[b::4])
        for k in range(1, 4):
            if b:
                c, s = math.cos(math.pi * b * k / 8.0), math.sin(math.pi * b * k / 8.0)
                re, im = column[k]
                column[k] = (re * c - im * s, re * s + im * c)
        first.append(column)
    last = [four([first[b][k] for b in range(4)]) for k in range(4)]
    return [last[k % 4][k // 4] for k in range(16)]


def depth_kernel(
    spec_ref, twist_hbm_ref, table_hbm_ref, out_ref, rows_ref, mid_ref, hold_ref, twist_ref, table_ref, sem, table_sem
):
    first = lax.axis_index("gy") * ROWS
    lane = lax.broadcasted_iota(jnp.int32, (16, INNER), 1)
    line = lax.broadcasted_iota(jnp.int32, (16, INNER), 0)

    def load(k):
        rows = pl.ds(pl.multiple_of(k * CHUNK, CHUNK), CHUNK)
        return pltpu.make_async_copy(spec_ref.at[:, rows, :], rows_ref.at[:, rows, :], sem.at[k])

    fetches = [
        pltpu.make_async_copy(twist_hbm_ref, twist_ref, table_sem.at[0]),
        pltpu.make_async_copy(table_hbm_ref, table_ref, table_sem.at[1]),
    ]
    fetches[0].start()
    for k in range(ROWS // CHUNK):
        load(k).start()
    fetches[1].start()
    fetches[0].wait()

    def rows_at(step, carry):
        at = pl.multiple_of(step * 16, 16)
        ky = first + at + line
        wy = jnp.where(2 * ky < NY, ky, ky - NY).astype(f32) * (2.0 * math.pi / NY)
        wy2 = wy * wy
        values = []
        for p in range(OUTER):
            kz = lane + p * INNER
            wz = jnp.where(2 * kz < NZ, kz, kz - NZ).astype(f32) * (2.0 * math.pi / NZ)
            base = 1.0 + CORRELATION * CORRELATION * (wy2 + wz * wz)
            gain = jnp.exp(jnp.log(base) * (-(HURST_EXPONENT + 1.0) / 2.0)) * (1.0 / math.sqrt(NY * NZ))
            span = pl.ds(p * INNER, INNER)
            values.append(
                (
                    rows_ref[0, pl.ds(at, 16), span].astype(f32) * gain,
                    rows_ref[1, pl.ds(at, 16), span].astype(f32) * gain,
                )
            )
        for q, (re, im) in enumerate(twelve(values)):
            c = twist_ref[pl.ds(2 * q, 1), :]
            s = twist_ref[pl.ds(2 * q + 1, 1), :]
            mid_ref[q, pl.ds(at, 16), pl.ds(0, INNER)] = (re * c - im * s).astype(bf16)
            mid_ref[q, pl.ds(at, 16), pl.ds(INNER, INNER)] = (re * s + im * c).astype(bf16)
        return carry

    def chunk(k, carry):
        load(k).wait()
        for i in range(CHUNK // 16):
            rows_at(k * (CHUNK // 16) + i, carry)
        return carry

    lax.fori_loop(0, ROWS // CHUNK, chunk, 0)
    fetches[1].wait()
    for q in range(OUTER):
        made = lax.dot_general(
            table_ref[...], mid_ref[q], (((1,), (1,)), ((), ())), preferred_element_type=f32
        )
        for half in range(2):
            for part in range(2):
                hold_ref[half, part, pl.ds(q, INNER, stride=OUTER), :] = made[
                    part * INNER : (part + 1) * INNER, half * 128 : (half + 1) * 128
                ]

    def pack(h, carry):
        for part in range(2):
            for b in range(0, BAND // DEEP, 2):
                for half in range(2):
                    two = [
                        hold_ref[half, part, pl.ds(pl.multiple_of((b + i) * PERIOD + h * DEEP, DEEP), DEEP), :]
                        for i in range(2)
                    ]
                    to = pl.ds(part * BAND + b * DEEP, 2 * DEEP)
                    out_ref[h, to, pl.ds(half * 128, 128)] = jnp.concatenate(two, axis=0).astype(bf16)
        return carry

    lax.fori_loop(0, GY, pack, 0, unroll=4)


def pieces(value):
    high = value.astype(bf16).astype(f32)
    rest = value - high
    middle = rest.astype(bf16).astype(f32)
    return high, middle, rest - middle


def y_kernel(
    y_bounds_ref, z_bounds_ref, in_ref, taper_ref, twist_ref, wave_hbm_ref, vp_ref, vs_ref, rho_ref,
    out_ref, vp_out_ref, vs_out_ref, rho_out_ref, mid_ref, field_ref, cut_ref, wave_ref, sem, wave_sem
):
    groups = LONG // ROWS
    models = ((vp_ref, vp_out_ref), (vs_ref, vs_out_ref), (rho_ref, rho_out_ref))
    fetches = [pltpu.make_async_copy(a, b, sem.at[k]) for k, (a, b) in enumerate(models)]
    waves = [pltpu.make_async_copy(wave_hbm_ref.at[k], wave_ref.at[k], wave_sem.at[k]) for k in range(LONG // 256)]
    for wave in waves:
        wave.start()

    def turn(low, carry):
        for row in range(0, BAND, 16):
            for col in range(0, ROWS, 128):
                values = []
                for e in range(RADIX):
                    block = groups * e + low
                    values.append(
                        (
                            in_ref[block, pl.ds(row, 16), pl.ds(col, 128)].astype(f32),
                            in_ref[block, pl.ds(BAND + row, 16), pl.ds(col, 128)].astype(f32),
                        )
                    )
                lanes = pl.multiple_of(low * ROWS + col, 128)
                for y1, (re, im) in enumerate(sixteen(values)):
                    c = twist_ref[low, pl.ds(2 * y1, 1), pl.ds(col, 128)]
                    s = twist_ref[low, pl.ds(2 * y1 + 1, 1), pl.ds(col, 128)]
                    at = pl.ds(y1 * BAND + row, 16)
                    mid_ref[at, pl.ds(lanes, 128)] = (re * c - im * s).astype(bf16)
                    mid_ref[at, pl.ds(pl.multiple_of(lanes + LONG, 128), 128)] = (re * s + im * c).astype(bf16)
        return carry

    lax.fori_loop(0, groups, turn, 0)
    total = jnp.zeros((8, 128), f32)
    taper = taper_ref[...]
    for block in range(LONG // 256):
        waves[block].wait()
        if block == len(waves) - 1:
            for fetch in fetches:
                fetch.start()
        made = jnp.dot(mid_ref[...], wave_ref[block], preferred_element_type=f32)
        for half in range(2):
            part = made[:, half * 128 : (half + 1) * 128] * taper
            field_ref[2 * block + half] = part
            total = total + jnp.sum((part * part).reshape(RADIX * BAND // 8, 8, 128), axis=0)
    sums = jnp.sum(jnp.sum(total, axis=0, keepdims=True), axis=1, keepdims=True)
    high, middle, low = pieces(jnp.broadcast_to(sums, (BAND, 128)))
    lane = lax.broadcasted_iota(jnp.int32, (BAND, 128), 1)
    extra = jnp.where(lane == 125, high, jnp.where(lane == 126, middle, jnp.where(lane == 127, low, 0.0)))
    for i in range(MANY):
        cut_ref[i, :, pl.ds(BAND, DEEP), :] = jnp.zeros((TILES, DEEP, 128), f32)
        cut_ref[i, TILES - 1, pl.ds(BAND, DEEP), :] = extra[:DEEP]
    here = lax.axis_index("gy") * DEEP
    tiles = [lax.div(z_bounds_ref[j] - here + (PERIOD - DEEP), PERIOD) * DEEP for j in range(GZ)]

    def window(g, place):
        y2_first = lax.div(y_bounds_ref[g], RADIX)
        block = lax.div(y2_first, 128)
        later = lax.rem(block + 1, LONG // 128)
        shift = lax.rem(y2_first, 128)
        before = lane < shift
        at = lane - shift + jnp.where(before, 128, 0)
        cut = jnp.minimum(lax.div(127 - shift, STEP), PER - 1)
        split = before & (at < STEP * (cut + 1))
        blocks = [jnp.where(i > cut, later, block) for i in range(PER)]
        for tile in range(TILES):
            parts = []
            for y1 in range(tile * PER, min(tile * PER + PER, RADIX)):
                parts.append(field_ref[blocks[y1 % PER], pl.ds(y1 * BAND, BAND), :])
            whole = parts[-1]
            for i in reversed(range(len(parts) - 1)):
                whole = jnp.where(at < STEP * (i + 1), parts[i], whole)
            other = jnp.minimum(tile * PER + cut, RADIX - 1)
            rows = pl.ds(pl.multiple_of(other * BAND, BAND), BAND)
            whole = jnp.where(split, field_ref[later, rows, :], whole)
            whole = pltpu.roll(whole, lax.rem(128 - shift, 128), 1)
            if tile == TILES - 1:
                whole = jnp.where(lane < STEP * len(parts), whole, extra)
            cut_ref[place, tile, pl.ds(0, BAND), :] = whole

    def send(g, place):
        for j in range(0, GZ, 2):
            to = pl.ds(pl.multiple_of((g * GZ + j) * DEEP, 2 * DEEP), 2 * DEEP)
            for tile in range(TILES):
                two = [cut_ref[place, tile, pl.ds(pl.multiple_of(tiles[j + i], DEEP), DEEP), :] for i in range(2)]
                out_ref[to, pl.ds(tile * 128, 128)] = jnp.concatenate(two, axis=0).astype(bf16)

    def several(k, carry):
        for i in range(MANY):
            window(k * MANY + i, i)
        for i in range(MANY):
            send(k * MANY + i, i)
        return carry

    lax.fori_loop(0, GY // MANY, several, 0)
    for fetch in fetches:
        fetch.wait()


def model_kernel(
    y_bounds_ref, z_bounds_ref, in_ref, vp_ref, vs_ref, rho_ref, new_vp_ref, new_vs_ref, new_rho_ref,
    made_ref, weave_ref, vp_out_ref, vs_out_ref, rho_out_ref, sem
):
    row, col = lax.axis_index("gy"), lax.axis_index("gz")
    y_first = y_bounds_ref[row]
    y_extent = y_bounds_ref[row + 1] - y_first
    z_first = z_bounds_ref[col]
    z_extent = z_bounds_ref[col + 1] - z_first
    group = X * DEEP
    tail = jnp.zeros((16, 128), f32)
    for k in range(GY * X * DEEP // 16):
        tail = tail + in_ref[pl.ds(16 * k, 16), pl.ds(WIDE - 128, 128)].astype(f32)
    first_row = lax.broadcasted_iota(jnp.int32, (16, 128), 0) % DEEP == 0
    first_row = first_row & (lax.broadcasted_iota(jnp.int32, (16, 128), 1) >= 125)
    total = jnp.sum(jnp.where(first_row, tail, 0.0), axis=0, keepdims=True)
    total = jnp.sum(total, axis=1, keepdims=True)
    factor = SPREAD_SIGMA / jnp.sqrt(total / (X * NY * NZ) + EPSILON)
    r = lax.broadcasted_iota(jnp.int32, (YCAP, WIDE), 0)
    col = lax.broadcasted_iota(jnp.int32, (YCAP, WIDE), 1)
    y = r + lax.rem(y_first, RADIX)
    y1 = y & (RADIX - 1)
    third = jnp.where(y1 >= 2 * PER, 2, jnp.where(y1 >= PER, 1, 0))
    wanted = third * 128 + (y1 - PER * third) * STEP + lax.div(y, RADIX)
    choose = jnp.where(col == wanted, 1.0, 0.0).astype(bf16)
    first = lax.div(lax.rem(z_first, PERIOD), DEEP)

    def natural(k):
        parts = []
        for i in range(4):
            h = lax.rem(first + 4 * k + i, GY)
            parts.append(in_ref[pl.ds(pl.multiple_of(h * group, group), group), :])
        made = lax.dot_general(
            choose, jnp.concatenate(parts, axis=0), (((1,), (1,)), ((), ())), preferred_element_type=f32
        )
        made_ref[:, pl.ds(k * 256, 256)] = made.astype(bf16)

    made_ref[:, pl.ds(GY * group, 128)] = jnp.zeros((YCAP, 128), bf16)
    source = lax.broadcasted_iota(jnp.int32, (WIDE, 256), 0)
    lane = lax.broadcasted_iota(jnp.int32, (WIDE, 256), 1)
    slot = (lane >> 3) + lax.rem(z_first, DEEP)
    wanted = (slot >> 3) * group + (lane & 7) * DEEP + (slot & 7)
    weave_ref[...] = jnp.where(source == wanted, 1.0, 0.0).astype(bf16)
    flat = X * ZCAP
    stores = []
    natural(0)
    for k in range(-(-flat // 256)):
        if k + 1 < GY // 4:
            natural(k + 1)
        wide = min(256, flat - 256 * k)
        span = pl.ds(k * 256, wide)
        planes = made_ref[:, pl.ds(k * 256, WIDE)]
        picked = jnp.dot(planes, weave_ref[...], preferred_element_type=f32)[:, :wide] * factor
        row = lax.broadcasted_iota(jnp.int32, (YCAP, wide), 0)
        slot = (lax.broadcasted_iota(jnp.int32, (YCAP, wide), 1) + k * 256) >> 3
        valid = (row < y_extent) & (slot < z_extent)
        vp_out_ref[:, span] = jnp.where(valid, vp_ref[:, span].astype(f32) * (1.0 + picked), 0.0)
        vs_out_ref[:, span] = jnp.where(valid, vs_ref[:, span].astype(f32) * (1.0 + picked), 0.0)
        rho_out_ref[:, span] = jnp.where(valid, rho_ref[:, span].astype(f32) * (1.0 + DENSITY_GAIN * picked), 0.0)
        pairs = ((vp_out_ref, new_vp_ref), (vs_out_ref, new_vs_ref), (rho_out_ref, new_rho_ref))
        for i, (a, b) in enumerate(pairs):
            stores.append(pltpu.make_async_copy(a.at[:, span], b.at[:, span], sem.at[i, k]))
            stores[-1].start()
    for store in stores:
        store.wait()


SMEM = pl.BlockSpec(memory_space=pltpu.SMEM)
VMEM = pl.BlockSpec(memory_space=pltpu.VMEM)
HBM = pl.BlockSpec(memory_space=pltpu.HBM)


def held(array):
    return pltpu.with_memory_space_constraint(array, pltpu.HBM)


def depth_stage(spec):
    return pl.pallas_call(
        depth_kernel,
        out_shape=pltpu.VMEM((GY, 2 * BAND, ROWS), bf16),
        in_specs=[HBM, HBM, HBM],
        out_specs=VMEM,
        scratch_shapes=[
            pltpu.VMEM((2, ROWS, NZ), bf16),
            pltpu.VMEM((OUTER, ROWS, 2 * INNER), bf16),
            pltpu.VMEM((2, 2, NZ, 128), f32),
            pltpu.VMEM((2 * OUTER, INNER), f32),
            pltpu.VMEM((2 * INNER, 2 * INNER), bf16),
            pltpu.SemaphoreType.DMA((ROWS // CHUNK,)),
            pltpu.SemaphoreType.DMA((2,)),
        ],
        compiler_params=pltpu.CompilerParams(vmem_limit_bytes=32 * MIB),
    )(held(spec), held(jnp.asarray(depth_twist())), held(jnp.asarray(inner_table())))


def y_stage(y_bounds, z_bounds, turned, taper, *models):
    return pl.pallas_call(
        y_kernel,
        out_shape=[pltpu.VMEM((GY * GZ * DEEP, WIDE), bf16)] + [pltpu.VMEM(m.shape, bf16) for m in models],
        in_specs=[SMEM, SMEM, VMEM, VMEM, VMEM, HBM, HBM, HBM, HBM],
        out_specs=[VMEM] * 4,
        scratch_shapes=[
            pltpu.VMEM((RADIX * BAND, 2 * LONG), bf16),
            pltpu.VMEM((LONG // 128, RADIX * BAND, 128), f32),
            pltpu.VMEM((MANY, TILES, BAND + DEEP, 128), f32),
            pltpu.VMEM((LONG // 256, 2 * LONG, 256), bf16),
            pltpu.SemaphoreType.DMA((3,)),
            pltpu.SemaphoreType.DMA((LONG // 256,)),
        ],
        compiler_params=pltpu.CompilerParams(vmem_limit_bytes=32 * MIB),
    )(y_bounds, z_bounds, turned, taper, y_twist(), held(jnp.asarray(y_table())), *[held(m) for m in models])


def model_stage(y_bounds, z_bounds, bricks, vp, vs, rho):
    flat = X * ZCAP
    whole = pltpu.VMEM((YCAP, flat), f32)
    return pl.pallas_call(
        model_kernel,
        out_shape=[jax.ShapeDtypeStruct((YCAP, flat), f32)] * 3,
        in_specs=[SMEM, SMEM, VMEM, VMEM, VMEM, VMEM],
        out_specs=[HBM] * 3,
        scratch_shapes=[
            pltpu.VMEM((YCAP, GY * X * DEEP + 128), bf16),
            pltpu.VMEM((WIDE, 256), bf16),
            whole,
            whole,
            whole,
            pltpu.SemaphoreType.DMA((3, -(-flat // 256))),
        ],
        compiler_params=pltpu.CompilerParams(vmem_limit_bytes=32 * MIB),
    )(y_bounds, z_bounds, bricks, vp, vs, rho)


def shards(spectrum, layer_index, y_bounds, z_bounds, vp, vs, rho):
    gy_index = lax.axis_index("gy")
    taper_all = (layer_index.astype(f32) + 1.0) / LAYERS
    taper_band = lax.dynamic_index_in_dim(taper_all.reshape(BAND // DEEP, GY, DEEP), gy_index, 1, False).reshape(BAND)
    taper = jnp.broadcast_to(jnp.tile(taper_band, RADIX)[:, None], (RADIX * BAND, 128))
    turned = depth_stage(spectrum.reshape(2, ROWS, NZ))
    turned = lax.all_to_all(turned, "gy", 0, 0, tiled=True)
    bricks, *models = y_stage(y_bounds, z_bounds, turned, taper, vp, vs, rho)
    bricks = lax.all_to_all(bricks.reshape(GY * GZ, DEEP, WIDE), ("gy", "gz"), 0, 0, tiled=True)
    bricks = bricks.reshape(GY * X * DEEP, WIDE)
    return tuple(model_stage(y_bounds, z_bounds, bricks, *models))


def solution(mesh):
    return jax.shard_map(
        shards,
        mesh=mesh,
        in_specs=(
            P(None, "gz", "gy", None),
            P(),
            P(),
            P(),
            P("gy", "gz"),
            P("gy", "gz"),
            P("gy", "gz"),
        ),
        out_specs=(P("gy", "gz"), P("gy", "gz"), P("gy", "gz")),
        check_vma=False,
    )
```

profile of v0, /device:TPU:1, one launch (start us, length us, event | category | flops | bytes accessed | tf_op | source)
XLA Modules:
  0.0 100.6 jit_solution(8713734700379718964)
XLA Ops:
  0.6 4.8 %shard_map.130 = bf16[32,96,256]{2,1,0:T(8,128)(2,1)} custom-call(bf16[2,256,1536]{2,1,0:T(8,128)(2,1)} %bitcast.5, f32[24,128]{1,0:T(8,128)} %constant.25.clone.twist_hbm_ref, bf16[256,256]{1,0:T(8,128)(2,1)} %constant.26.clone.table_hbm_ref), custom_call_target="tpu_custom_call" | custom-call | tf_op jit(solution)/shard_map/pallas_call | solution.py:366
  5.5 0.0 copy-start.3
  5.5 0.0 copy-start
  5.5 0.0 copy-start.1
  5.5 0.0 copy-start.2
  5.5 8.7 %all-to-all-start = ((bf16[32,96,256]{2,1,0:T(8,128)(2,1)}), bf16[32,96,256]{2,1,0:T(8,128)(2,1)S(1)}, u32[]{:S(2)}, u32[]{:S(2)}) async-start(bf16[32,96,256]{2,1,0:T(8,128)(2,1)} %shard_map.130), calls=%async_computation | async-start | bytes 3145728 | tf_op jit(solution)/shard_map/all_to_all | solution.py:428
  14.2 0.0 copy-done.3
  14.3 0.1 reshape.22
  14.4 0.1 tile.7
  14.5 0.1 broadcast_in_dim.7
  14.6 22.4 %all-to-all-done.in_ref = bf16[32,96,256]{2,1,0:T(8,128)(2,1)S(1)} async-done(((bf16[32,96,256]{2,1,0:T(8,128)(2,1)}), bf16[32,96,256]{2,1,0:T(8,128)(2,1)S(1)}, u32[]{:S(2)}, u32[]{:S(2)}) %all-to-all-start) | async-done | bytes 1572896 | tf_op jit(solution)/shard_map/all_to_all | solution.py:428
  36.9 0.2 broadcast_in_dim.8.taper_ref
  37.1 0.0 copy-done
  37.1 0.0 copy-done.1
  37.1 0.0 copy-done.2
  37.1 5.3 %shard_map.131 = (bf16[2048,384]{1,0:T(8,128)(2,1)S(1)}, bf16[320,1920]{1,0:T(8,128)(2,1)S(1)}, bf16[320,1920]{1,0:T(8,128)(2,1)S(1)}, bf16[320,1920]{1,0:T(8,128)(2,1)S(1)}) custom-call(s32[33]{0:T(128)S(1)} %copy-done.1, s32[9]{0:T(128)S(1)} %copy-done.2, bf16[32,96,256]{2,1,0:T(8,128)(2,1)S(1)} %all-to-all-done.in_ref, ...), custom_call_target="tpu_custom_call" | custom-call | tf_op jit(solution)/shard_map/pallas_call | solution.py:385
  42.4 53.7 %all_to_all.10 = bf16[256,8,384]{2,1,0:T(8,128)(2,1)S(1)} all-to-all(bf16[256,8,384]{2,1,0:T(8,128)(2,1)S(1)} %bitcast.4), channel_id=1, replica_groups=mesh['gy'=32,'gz'=8] {'gy','gz'}, dimensions={0} | all-to-all | bytes 3145728 | tf_op jit(solution)/shard_map/all_to_all | solution.py:430
  96.1 4.5 %shard_map.132 = (f32[320,1920]{1,0:T(8,128)}, f32[320,1920]{1,0:T(8,128)}, f32[320,1920]{1,0:T(8,128)}) custom-call(s32[33]{0:T(128)S(1)} %copy-done.1, s32[9]{0:T(128)S(1)} %copy-done.2, bf16[2048,384]{1,0:T(8,128)(2,1)S(1)} %bitcast.3, bf16[320,1920]{1,0:T(8,128)(2,1)S(1)} %get-tuple-element.8.vp_ref, bf16[320,1920]{1,0:T(8,128)(2,1)S(1)} %get-tuple-element.9.vs_ref, ...), custom_call_target="tpu_custom_call" | custom-call | tf_op jit(solution)/shard_map/pallas_call | solution.py:405
  (3 shorter events, 0.0 us)
Async XLA Ops:
  5.5 8.8 %copy-start.3 = (s32[1536]{0:T(1024)S(1)}, s32[1536]{0:T(1024)}, u32[]{:S(2)}) copy-start(s32[1536]{0:T(1024)} %param.12) | copy-start | bytes 18436
  5.5 31.6 %copy-start = (f32[2,32,256]{2,1,0:T(8,128)S(1)}, f32[2,32,256]{2,1,0:T(8,128)}, u32[]{:S(2)}) copy-start(f32[2,32,256]{2,1,0:T(8,128)} %constant.28.clone.twist_ref) | copy-start | bytes 196612
  5.5 31.6 %copy-start.1 = (s32[33]{0:T(128)S(1)}, s32[33]{0:T(128)}, u32[]{:S(2)}) copy-start(s32[33]{0:T(128)} %y_bounds_ref.3) | copy-start | bytes 400
  5.5 31.6 %copy-start.2 = (s32[9]{0:T(128)S(1)}, s32[9]{0:T(128)}, u32[]{:S(2)}) copy-start(s32[9]{0:T(128)} %z_bounds_ref.3) | copy-start | bytes 112
  5.5 31.4 %all-to-all-start = ((bf16[32,96,256]{2,1,0:T(8,128)(2,1)}), bf16[32,96,256]{2,1,0:T(8,128)(2,1)S(1)}, u32[]{:S(2)}, u32[]{:S(2)}) async-start(bf16[32,96,256]{2,1,0:T(8,128)(2,1)} %shard_map.130), calls=%async_computation | async-start | bytes 3145728 | tf_op jit(solution)/shard_map/all_to_all | solution.py:428
where the time goes:
time: 101 us
  blocking collectives  53.7 us (53%)
  waiting for transfers between devices  22.4 us (22%)
  Pallas kernels  14.6 us (14%)
  starting transfers between devices  8.73 us (9%)
    all_to_all x1, blocking collectives, shards(): lax.all_to_all(bricks.reshape(GY * GZ, DEEP, WIDE), ('gy', 'gz'), 0, 0, t...  53.7 us
    all_to_all x1, waiting for transfers between devices, shards(): turned = lax.all_to_all(turned, 'gy', 0, 0, tiled=True)  22.4 us
    all_to_all x1, starting transfers between devices, shards(): turned = lax.all_to_all(turned, 'gy', 0, 0, tiled=True)  8.73 us
    pallas_call x1, Pallas kernels, y_stage(): pl.pallas_call(y_kernel, out_shape=[pltpu.VMEM((GY * GZ * DEEP, WIDE), bf...  5.3 us
    pallas_call x1, Pallas kernels, depth_stage(): pl.pallas_call(depth_kernel, out_shape=pltpu.VMEM((GY, 2 * BAND, ROWS), b...  4.82 us
    pallas_call x1, Pallas kernels, model_stage(): pl.pallas_call(model_kernel, out_shape=[jax.ShapeDtypeStruct((YCAP, flat)...  4.46 us
  transfers between devices with their start and end apart: 1, of which 1 were waited for; matrix products, arithmetic and copies ran while one was open for 0% of the time, Pallas kernels for 0%

commit v1 on v0

--- a/solution.py
+++ b/solution.py
@@ -29,7 +29,7 @@
 STEP = YCAP // RADIX + 1
 PER = 6
 WIDE = 384
-MANY = 8
+MANY = 16
 TILES = WIDE // 128
 DEEP = 8
 PERIOD = GY * DEEP
@@ -102,7 +102,7 @@
 
 
 def depth_kernel(
-    spec_ref, twist_hbm_ref, table_hbm_ref, out_ref, rows_ref, mid_ref, hold_ref, twist_ref, table_ref, sem, table_sem
+    spec_ref, twist_hbm_ref, table_hbm_ref, wave_ref, out_ref, wave_out_ref, rows_ref, mid_ref, hold_ref, twist_ref, table_ref, sem, table_sem
 ):
     first = lax.axis_index("gy") * ROWS
     lane = lax.broadcasted_iota(jnp.int32, (16, INNER), 1)
@@ -115,11 +115,13 @@
     fetches = [
         pltpu.make_async_copy(twist_hbm_ref, twist_ref, table_sem.at[0]),
         pltpu.make_async_copy(table_hbm_ref, table_ref, table_sem.at[1]),
+        pltpu.make_async_copy(wave_ref, wave_out_ref, table_sem.at[2]),
     ]
     fetches[0].start()
     for k in range(ROWS // CHUNK):
         load(k).start()
     fetches[1].start()
+    fetches[2].start()
     fetches[0].wait()
 
     def rows_at(step, carry):
@@ -178,6 +180,7 @@
         return carry
 
     lax.fori_loop(0, GY, pack, 0, unroll=4)
+    fetches[2].wait()
 
 
 def pieces(value):
@@ -188,15 +191,14 @@
 
 
 def y_kernel(
-    y_bounds_ref, z_bounds_ref, in_ref, taper_ref, twist_ref, wave_hbm_ref, vp_ref, vs_ref, rho_ref,
-    out_ref, vp_out_ref, vs_out_ref, rho_out_ref, mid_ref, field_ref, cut_ref, wave_ref, sem, wave_sem
+    y_bounds_ref, z_bounds_ref, in_ref, taper_ref, twist_ref, wave_ref, vp_ref, vs_ref, rho_ref,
+    out_ref, vp_out_ref, vs_out_ref, rho_out_ref, mid_ref, field_ref, cut_ref, sem
 ):
     groups = LONG // ROWS
     models = ((vp_ref, vp_out_ref), (vs_ref, vs_out_ref), (rho_ref, rho_out_ref))
     fetches = [pltpu.make_async_copy(a, b, sem.at[k]) for k, (a, b) in enumerate(models)]
-    waves = [pltpu.make_async_copy(wave_hbm_ref.at[k], wave_ref.at[k], wave_sem.at[k]) for k in range(LONG // 256)]
-    for wave in waves:
-        wave.start()
+    for fetch in fetches:
+        fetch.start()
 
     def turn(low, carry):
         for row in range(0, BAND, 16):
@@ -223,10 +225,6 @@
     total = jnp.zeros((8, 128), f32)
     taper = taper_ref[...]
     for block in range(LONG // 256):
-        waves[block].wait()
-        if block == len(waves) - 1:
-            for fetch in fetches:
-                fetch.start()
         made = jnp.dot(mid_ref[...], wave_ref[block], preferred_element_type=f32)
         for half in range(2):
             part = made[:, half * 128 : (half + 1) * 128] * taper
@@ -362,12 +360,12 @@
     return pltpu.with_memory_space_constraint(array, pltpu.HBM)
 
 
-def depth_stage(spec):
+def depth_stage(spec, wave):
     return pl.pallas_call(
         depth_kernel,
-        out_shape=pltpu.VMEM((GY, 2 * BAND, ROWS), bf16),
-        in_specs=[HBM, HBM, HBM],
-        out_specs=VMEM,
+        out_shape=[pltpu.VMEM((GY, 2 * BAND, ROWS), bf16), pltpu.VMEM(wave.shape, bf16)],
+        in_specs=[HBM, HBM, HBM, HBM],
+        out_specs=[VMEM, VMEM],
         scratch_shapes=[
             pltpu.VMEM((2, ROWS, NZ), bf16),
             pltpu.VMEM((OUTER, ROWS, 2 * INNER), bf16),
@@ -375,28 +373,26 @@
             pltpu.VMEM((2 * OUTER, INNER), f32),
             pltpu.VMEM((2 * INNER, 2 * INNER), bf16),
             pltpu.SemaphoreType.DMA((ROWS // CHUNK,)),
-            pltpu.SemaphoreType.DMA((2,)),
+            pltpu.SemaphoreType.DMA((3,)),
         ],
         compiler_params=pltpu.CompilerParams(vmem_limit_bytes=32 * MIB),
-    )(held(spec), held(jnp.asarray(depth_twist())), held(jnp.asarray(inner_table())))
-
-
-def y_stage(y_bounds, z_bounds, turned, taper, *models):
+    )(held(spec), held(jnp.asarray(depth_twist())), held(jnp.asarray(inner_table())), held(wave))
+
+
+def y_stage(y_bounds, z_bounds, turned, taper, wave, *models):
     return pl.pallas_call(
         y_kernel,
         out_shape=[pltpu.VMEM((GY * GZ * DEEP, WIDE), bf16)] + [pltpu.VMEM(m.shape, bf16) for m in models],
-        in_specs=[SMEM, SMEM, VMEM, VMEM, VMEM, HBM, HBM, HBM, HBM],
+        in_specs=[SMEM, SMEM, VMEM, VMEM, VMEM, VMEM, HBM, HBM, HBM],
         out_specs=[VMEM] * 4,
         scratch_shapes=[
             pltpu.VMEM((RADIX * BAND, 2 * LONG), bf16),
             pltpu.VMEM((LONG // 128, RADIX * BAND, 128), f32),
             pltpu.VMEM((MANY, TILES, BAND + DEEP, 128), f32),
-            pltpu.VMEM((LONG // 256, 2 * LONG, 256), bf16),
             pltpu.SemaphoreType.DMA((3,)),
-            pltpu.SemaphoreType.DMA((LONG // 256,)),
         ],
         compiler_params=pltpu.CompilerParams(vmem_limit_bytes=32 * MIB),
-    )(y_bounds, z_bounds, turned, taper, y_twist(), held(jnp.asarray(y_table())), *[held(m) for m in models])
+    )(y_bounds, z_bounds, turned, taper, y_twist(), wave, *[held(m) for m in models])
 
 
 def model_stage(y_bounds, z_bounds, bricks, vp, vs, rho):
@@ -424,9 +420,9 @@
     taper_all = (layer_index.astype(f32) + 1.0) / LAYERS
     taper_band = lax.dynamic_index_in_dim(taper_all.reshape(BAND // DEEP, GY, DEEP), gy_index, 1, False).reshape(BAND)
     taper = jnp.broadcast_to(jnp.tile(taper_band, RADIX)[:, None], (RADIX * BAND, 128))
-    turned = depth_stage(spectrum.reshape(2, ROWS, NZ))
+    turned, wave = depth_stage(spectrum.reshape(2, ROWS, NZ), jnp.asarray(y_table()))
     turned = lax.all_to_all(turned, "gy", 0, 0, tiled=True)
-    bricks, *models = y_stage(y_bounds, z_bounds, turned, taper, vp, vs, rho)
+    bricks, *models = y_stage(y_bounds, z_bounds, turned, taper, wave, vp, vs, rho)
     bricks = lax.all_to_all(bricks.reshape(GY * GZ, DEEP, WIDE), ("gy", "gz"), 0, 0, tiled=True)
     bricks = bricks.reshape(GY * X * DEEP, WIDE)
     return tuple(model_stage(y_bounds, z_bounds, bricks, *models))

time: 101 us -> 99.7 us (0.987)
  Pallas kernels: 14.6 us -> 13.5 us
    pallas_call x1, Pallas kernels: 5.3 us -> 4.2 us  [y_stage(): pl.pallas_call(y_kernel, out_shape=[pltpu.VMEM((GY * GZ * DEEP, WIDE), bf...]
where the time goes in v1:
time: 99.7 us; the launch traced here: 99.5 us
  blocking collectives  53.7 us (54%)
  waiting for transfers between devices  22.4 us (22%)
  Pallas kernels  13.5 us (14%)
  starting transfers between devices  8.73 us (9%)
    all_to_all x1, blocking collectives, shards(): lax.all_to_all(bricks.reshape(GY * GZ, DEEP, WIDE), ('gy', 'gz'), 0, 0, t...  53.7 us
    all_to_all x1, waiting for transfers between devices, shards(): turned = lax.all_to_all(turned, 'gy', 0, 0, tiled=True)  22.4 us
    all_to_all x1, starting transfers between devices, shards(): turned = lax.all_to_all(turned, 'gy', 0, 0, tiled=True)  8.73 us
    pallas_call x1, Pallas kernels, depth_stage(): pl.pallas_call(depth_kernel, out_shape=[pltpu.VMEM((GY, 2 * BAND, ROWS),...  4.8 us
    pallas_call x1, Pallas kernels, model_stage(): pl.pallas_call(model_kernel, out_shape=[jax.ShapeDtypeStruct((YCAP, flat)...  4.46 us
    pallas_call x1, Pallas kernels, y_stage(): pl.pallas_call(y_kernel, out_shape=[pltpu.VMEM((GY * GZ * DEEP, WIDE), bf...  4.2 us
  transfers between devices with their start and end apart: 1, of which 1 were waited for; matrix products, arithmetic and copies ran while one was open for 0% of the time, Pallas kernels for 0%

profile of v1, /device:TPU:1, one launch (start us, length us, event | category | flops | bytes accessed | tf_op | source)
XLA Modules:
  0.0 99.5 jit_solution(5589416368473289526)
XLA Ops:
  0.6 4.8 %shard_map.130 = (bf16[32,96,256]{2,1,0:T(8,128)(2,1)}, bf16[2,1024,256]{2,1,0:T(8,128)(2,1)S(1)}) custom-call(bf16[2,256,1536]{2,1,0:T(8,128)(2,1)} %bitcast.5, f32[24,128]{1,0:T(8,128)} %constant.26.clone.twist_hbm_ref, bf16[256,256]{1,0:T(8,128)(2,1)} %constant.27.clone.table_hbm_ref, bf16[2,1024,256]{2,1,0:T(8,128)(2,1)} %constant.25.clone.wave_ref), custom_call_target="tpu_custom_call" | custom-call | tf_op jit(solution)/shard_map/pallas_call | solution.py:364
  5.4 0.0 copy-start.3
  5.4 0.0 copy-start
  5.5 0.0 copy-start.1
  5.5 0.0 copy-start.2
  5.5 8.7 %all-to-all-start = ((bf16[32,96,256]{2,1,0:T(8,128)(2,1)}), bf16[32,96,256]{2,1,0:T(8,128)(2,1)S(1)}, u32[]{:S(2)}, u32[]{:S(2)}) async-start(bf16[32,96,256]{2,1,0:T(8,128)(2,1)} %get-tuple-element.9), calls=%async_computation | async-start | bytes 3145728 | tf_op jit(solution)/shard_map/all_to_all | solution.py:424
  14.2 0.0 copy-done.3
  14.2 0.1 reshape.22
  14.4 0.1 tile.7
  14.5 0.1 broadcast_in_dim.7
  14.5 22.4 %all-to-all-done.in_ref = bf16[32,96,256]{2,1,0:T(8,128)(2,1)S(1)} async-done(((bf16[32,96,256]{2,1,0:T(8,128)(2,1)}), bf16[32,96,256]{2,1,0:T(8,128)(2,1)S(1)}, u32[]{:S(2)}, u32[]{:S(2)}) %all-to-all-start) | async-done | bytes 1572896 | tf_op jit(solution)/shard_map/all_to_all | solution.py:424
  36.9 0.2 broadcast_in_dim.8.taper_ref
  37.1 0.0 copy-done
  37.1 0.0 copy-done.1
  37.1 0.0 copy-done.2
  37.1 4.2 %shard_map.131 = (bf16[2048,384]{1,0:T(8,128)(2,1)S(1)}, bf16[320,1920]{1,0:T(8,128)(2,1)S(1)}, bf16[320,1920]{1,0:T(8,128)(2,1)S(1)}, bf16[320,1920]{1,0:T(8,128)(2,1)S(1)}) custom-call(s32[33]{0:T(128)S(1)} %copy-done.1, s32[9]{0:T(128)S(1)} %copy-done.2, bf16[32,96,256]{2,1,0:T(8,128)(2,1)S(1)} %all-to-all-done.in_ref, ...), custom_call_target="tpu_custom_call" | custom-call | tf_op jit(solution)/shard_map/pallas_call | solution.py:383
  41.3 53.7 %all_to_all.10 = bf16[256,8,384]{2,1,0:T(8,128)(2,1)S(1)} all-to-all(bf16[256,8,384]{2,1,0:T(8,128)(2,1)S(1)} %bitcast.4), channel_id=1, replica_groups=mesh['gy'=32,'gz'=8] {'gy','gz'}, dimensions={0} | all-to-all | bytes 3145728 | tf_op jit(solution)/shard_map/all_to_all | solution.py:426
  95.0 4.5 %shard_map.132 = (f32[320,1920]{1,0:T(8,128)}, f32[320,1920]{1,0:T(8,128)}, f32[320,1920]{1,0:T(8,128)}) custom-call(s32[33]{0:T(128)S(1)} %copy-done.1, s32[9]{0:T(128)S(1)} %copy-done.2, bf16[2048,384]{1,0:T(8,128)(2,1)S(1)} %bitcast.3, bf16[320,1920]{1,0:T(8,128)(2,1)S(1)} %get-tuple-element.12.vp_ref, bf16[320,1920]{1,0:T(8,128)(2,1)S(1)} %get-tuple-element.13.vs_ref, ...), custom_call_target="tpu_custom_call" | custom-call | tf_op jit(solution)/shard_map/pallas_call | solution.py:401
  (3 shorter events, 0.0 us)
Async XLA Ops:
  5.4 8.8 %copy-start.3 = (s32[1536]{0:T(1024)S(1)}, s32[1536]{0:T(1024)}, u32[]{:S(2)}) copy-start(s32[1536]{0:T(1024)} %param.12) | copy-start | bytes 18436
  5.4 31.6 %copy-start = (f32[2,32,256]{2,1,0:T(8,128)S(1)}, f32[2,32,256]{2,1,0:T(8,128)}, u32[]{:S(2)}) copy-start(f32[2,32,256]{2,1,0:T(8,128)} %constant.28.clone.twist_ref) | copy-start | bytes 196612
  5.5 31.6 %copy-start.1 = (s32[33]{0:T(128)S(1)}, s32[33]{0:T(128)}, u32[]{:S(2)}) copy-start(s32[33]{0:T(128)} %y_bounds_ref.3) | copy-start | bytes 400
  5.5 31.6 %copy-start.2 = (s32[9]{0:T(128)S(1)}, s32[9]{0:T(128)}, u32[]{:S(2)}) copy-start(s32[9]{0:T(128)} %z_bounds_ref.3) | copy-start | bytes 112
  5.5 31.4 %all-to-all-start = ((bf16[32,96,256]{2,1,0:T(8,128)(2,1)}), bf16[32,96,256]{2,1,0:T(8,128)(2,1)S(1)}, u32[]{:S(2)}, u32[]{:S(2)}) async-start(bf16[32,96,256]{2,1,0:T(8,128)(2,1)} %get-tuple-element.9), calls=%async_computation | async-start | bytes 3145728 | tf_op jit(solution)/shard_map/all_to_all | solution.py:424
